TPU v7x, 512 devices: a whole 4x8x8 slice. The times are simulated.
512 devices in a mesh: attn: 16 (over z, x_hi), exp: 32 (over x_lo, y, core).
Axes of the slice: x: 4 (x_hi: 2, x_lo: 2; x = x_hi * 2 + x_lo), y: 8, z: 8, core: 2. Of those that a mesh axis runs over, the one named last changes fastest.
Arguments:
- residual: bfloat16 [4096, 2880], P(('exp', 'attn')), may hold values from -16 to 16
- queries: bfloat16 [4096, 2048], P(('exp', 'attn')), may hold values from -6 to 6
- window_key_value_cache: bfloat16 [4096, 4, 128, 128], P(('exp', 'attn')), may hold values from -6 to 6
- new_key_value: bfloat16 [4096, 4, 128], P(('exp', 'attn')), may hold values from -5.5 to 5.5
- head_sink_logits: float32 [32], replicated, may hold values from 0 to 5
- out_proj: bfloat16 [2048, 2880], P('attn'), may hold values from -0.125 to 0.125
- norm_gain: float32 [2880], replicated, may hold values from 0.5 to 1.5
- expert_ids: int32 [4096, 4], P('exp'), may hold values from 0 to 31, as said below
- gate_mix: float32 [4096, 4], P('exp'), may hold values from 0.05 to 0.6
- w_gate: bfloat16 [32, 2880, 2880], P('exp', None, 'attn'), may hold values from -0.109375 to 0.109375
- w_up: bfloat16 [32, 2880, 2880], P('exp', None, 'attn'), may hold values from -0.109375 to 0.109375
- w_down: bfloat16 [32, 2880, 2880], P('exp', 'attn'), may hold values from -0.109375 to 0.109375
Outputs:
- layer_out: bfloat16 [4096, 2880], P(('exp', 'attn'))
Inputs may be any that keep to these rules, and one draw needn't show every extreme that they name: `expert_ids`: each row names 4 different experts. Within the rows of one index of exp (aligned blocks of 128 rows) no expert is named more than 32 times, and one expert is named exactly 32 times in every block.
All inputs are finite; a program needn't handle non-finite values.
Results may differ from a plain program's by a relative error of at most 0.02.
Values may be sent and summed in bfloat16 or wider, within the bound.
No kernel may reach another device: no remote copies, remote signals or barrier semaphores. Data moves between devices by JAX's collectives and lax.ppermute only.
A program may use at most 128 MiB of HBM per device.

v0:
```python
import jax
import jax.numpy as jnp
from jax import lax
from jax.sharding import PartitionSpec as P

HEAD_SIZE = 64
QUERY_HEADS = 32
KEY_VALUE_HEADS = 4


def attend(queries, window_key_value_cache, new_key_value, head_sink_logits):
    count_of_rows = queries.shape[0]
    query_groups = QUERY_HEADS // KEY_VALUE_HEADS
    grouped_queries = queries.reshape(count_of_rows, KEY_VALUE_HEADS, query_groups, HEAD_SIZE)
    all_keys = jnp.concatenate(
        [window_key_value_cache[:, :, :, :HEAD_SIZE], new_key_value[:, :, None, :HEAD_SIZE]], axis=2
    )
    all_values = jnp.concatenate(
        [window_key_value_cache[:, :, :, HEAD_SIZE:], new_key_value[:, :, None, HEAD_SIZE:]], axis=2
    )
    scores = jnp.einsum(
        "rkgd,rkjd->rkgj", grouped_queries, all_keys, preferred_element_type=jnp.float32
    ) * HEAD_SIZE ** (-0.5)
    sink_portion = head_sink_logits.reshape(1, KEY_VALUE_HEADS, query_groups, 1)
    highest = jnp.maximum(jnp.max(scores, axis=3, keepdims=True), sink_portion)
    raised = jnp.exp(scores - highest)
    denominator = jnp.sum(raised, axis=3, keepdims=True) + jnp.exp(sink_portion - highest)
    weights = (raised / denominator).astype(jnp.bfloat16)
    combined = jnp.einsum(
        "rkgj,rkjd->rkgd", weights, all_values, preferred_element_type=jnp.float32
    )
    return combined.reshape(count_of_rows, QUERY_HEADS * HEAD_SIZE).astype(jnp.bfloat16)


def run_experts(row_block, w_gate, w_up, w_down):
    sources, slot_count, width = row_block.shape
    local_experts = w_gate.shape[0]
    grouped_queries = row_block.reshape(sources // local_experts, local_experts, slot_count, width)
    gate_proj = jnp.einsum(
        "sjcd,jdf->sjcf", grouped_queries, w_gate, preferred_element_type=jnp.float32
    )
    up_proj = jnp.einsum(
        "sjcd,jdf->sjcf", grouped_queries, w_up, preferred_element_type=jnp.float32
    )
    activated = (gate_proj * jax.nn.sigmoid(1.702 * gate_proj) * (up_proj + 1.0)).astype(
        jnp.bfloat16
    )
    partial_value = jnp.einsum(
        "sjcf,jfd->sjcd", activated, w_down, preferred_element_type=jnp.float32
    ).astype(jnp.bfloat16)
    return partial_value.reshape(sources, slot_count, width)


def local(
    residual,
    queries,
    window_key_value_cache,
    new_key_value,
    head_sink_logits,
    out_proj,
    norm_gain,
    expert_ids,
    gate_mix,
    w_gate,
    w_up,
    w_down,
):
    column_rows, top_count = expert_ids.shape
    expert_total = w_gate.shape[0] * lax.axis_size("exp")
    capacity = 2 * column_rows * top_count // expert_total
    attention_output = attend(queries, window_key_value_cache, new_key_value, head_sink_logits)
    head_slices = lax.all_to_all(attention_output, "attn", split_axis=1, concat_axis=0, tiled=True)
    hidden_state = residual.astype(jnp.float32) + lax.psum_scatter(
        jnp.dot(head_slices, out_proj, preferred_element_type=jnp.float32).astype(jnp.bfloat16),
        "attn",
        scatter_dimension=0,
        tiled=True,
    ).astype(jnp.float32)
    mean_square = jnp.mean(hidden_state * hidden_state, axis=1, keepdims=True)
    normed = (hidden_state * lax.rsqrt(mean_square + 1e-05) * norm_gain).astype(jnp.bfloat16)
    flat_ids = expert_ids.reshape(-1)
    onehot_table = (flat_ids[:, None] == jnp.arange(expert_total, dtype=jnp.int32)[None, :]).astype(
        jnp.int32
    )
    slot_index = jnp.sum((jnp.cumsum(onehot_table, axis=0) - 1) * onehot_table, axis=1)
    places = flat_ids * capacity + slot_index
    row_number = jnp.arange(column_rows * top_count, dtype=jnp.int32) // top_count
    source_rows = (
        jnp.full((expert_total * capacity,), column_rows, jnp.int32).at[places].set(row_number)
    )
    column = lax.all_gather(normed, "attn", axis=0, tiled=True)
    padded = jnp.concatenate([column, jnp.zeros((1, column.shape[1]), jnp.bfloat16)], axis=0)
    outgoing = jnp.take(padded, source_rows, axis=0).reshape(
        expert_total, capacity, column.shape[1]
    )
    partial_value = run_experts(
        lax.all_to_all(outgoing, "exp", split_axis=0, concat_axis=0, tiled=True),
        w_gate,
        w_up,
        w_down,
    )
    returned = lax.all_to_all(partial_value, "exp", split_axis=0, concat_axis=0, tiled=True)
    picked = jnp.take(returned.reshape(expert_total * capacity, returned.shape[2]), places, axis=0)
    weighted = jnp.sum(
        picked.reshape(column_rows, top_count, picked.shape[1]).astype(jnp.float32)
        * gate_mix[:, :, None],
        axis=1,
    )
    combined = lax.psum_scatter(
        weighted.astype(jnp.bfloat16), "attn", scatter_dimension=0, tiled=True
    ).astype(jnp.float32)
    return (hidden_state + combined).astype(jnp.bfloat16)


def solution(mesh):
    in_specs = (
        P(("exp", "attn"), None),
        P(("exp", "attn"), None),
        P(("exp", "attn"), None, None, None),
        P(("exp", "attn"), None, None),
        P(),
        P("attn", None),
        P(),
        P("exp", None),
        P("exp", None),
        P("exp", None, "attn"),
        P("exp", None, "attn"),
        P("exp", "attn", None),
    )
    out_specs = P(("exp", "attn"), None)
    return jax.shard_map(local, mesh=mesh, in_specs=in_specs, out_specs=out_specs, check_vma=False)
```

profile of v0, /device:TPU:8, one launch (start us, length us, event | category | flops | bytes accessed | tf_op | source)
XLA Modules:
  0.0 752.3 jit_solution(5121819863465048144)
XLA Ops:
  6.5 0.9 fusion.42
  7.4 1.1 copy.43
  8.5 2.2 fusion.41
  10.7 1.2 copy.55
  11.9 0.1 reshape.140
  12.0 0.1 max.18
  12.1 0.3 copy.46
  12.4 0.4 copy.57
  12.9 1.6 fusion.43
  14.5 0.2 fusion.24
  14.8 0.4 convolution_convert_fusion.2
  15.2 0.1 convert_element_type.51
  15.3 0.6 copy.47
  15.9 12.9 %all-to-all-start = ((bf16[8,16,128]{2,0,1:T(8,128)(2,1)}), bf16[8,16,128]{2,0,1:T(8,128)(2,1)S(1)}, u32[]{:S(2)}, u32[]{:S(2)}) async-start(bf16[8,16,128]{2,0,1:T(8,128)(2,1)} %copy.47), calls=%async_computation | async-start | bytes 65536 | tf_op jit(solution)/shard_map/all_to_all | solution.py:72
  28.9 0.1 copy.48
  29.0 0.1 eq.26
  29.1 0.1 reshape.141
  29.3 1.2 reduce-window.6
  30.4 0.2 slice_reduce_fusion
  30.7 0.1 copy.53
  30.8 0.1 mul.76
  30.9 0.1 fusion.28
  31.0 8.1 %all-to-all-done = bf16[8,16,128]{2,0,1:T(8,128)(2,1)S(1)} async-done(((bf16[8,16,128]{2,0,1:T(8,128)(2,1)}), bf16[8,16,128]{2,0,1:T(8,128)(2,1)S(1)}, u32[]{:S(2)}, u32[]{:S(2)}) %all-to-all-start) | async-done | bytes 32800 | tf_op jit(solution)/shard_map/all_to_all | solution.py:72
  39.1 1.2 convolution_convert_fusion.1
  40.4 2.4 scatter_custom_fusion
  42.9 0.1 broadcast_in_dim.45
  43.0 1.3 dynamic-slice
  44.9 154.8 %all-reduce.6.cloned.1.call-done = bf16[128,2880]{1,0:T(8,128)(2,1)} async-done(((bf16[128,2880]{1,0:T(8,128)(2,1)}), bf16[128,2880]{1,0:T(8,128)(2,1)}) %all-reduce.6.cloned.1.call-update) | async-done | bytes 737296
  199.7 0.9 multiply_reduce_fusion.1
  200.6 0.9 multiply_convert_fusion
  201.5 44.4 %all_gather.3 = bf16[128,2880]{1,0:T(8,128)(2,1)S(1)} all-gather(bf16[8,2880]{1,0:T(8,128)(2,1)S(1)} %multiply_convert_fusion), channel_id=1, replica_groups=mesh['attn'=16,'exp'=32] {'attn'}, dimensions={0}, use_global_device_ids=true | all-gather | bytes 783360 | tf_op jit(solution)/shard_map/all_gather | solution.py:91
  246.0 6.5 gather_fusion
  252.6 3.4 broadcast_select_fusion
  256.0 143.5 %all_to_all.26 = bf16[32,32,2880]{2,1,0:T(8,128)(2,1)S(1)} all-to-all(bf16[32,32,2880]{2,1,0:T(8,128)(2,1)S(1)} %broadcast_select_fusion), channel_id=1, replica_groups=mesh['attn'=16,'exp'=32] {'exp'}, dimensions={0} | all-to-all | bytes 11796480 | tf_op jit(solution)/shard_map/all_to_all | solution.py:97
  399.5 2.6 copy-done.1
  402.1 2.8 convolution_bitcast_fusion
  404.9 12.4 %convolution_convert_fusion = bf16[32,32,2880]{2,1,0:T(8,128)(2,1)} fusion(bf16[32,32,2880]{2,1,0:T(8,128)(2,1)} %copy-done.1, bf16[1,180,2880]{2,1,0:T(8,128)(2,1)S(1)} %copy-done, bf16[1,2880,180]{1,2,0:T(8,128)(2,1)} %param.22, f32[32,1,32,180]{3,2,0,1:T(8,128)} %convolution_bitcast_fusion), kind=kOutput, calls=%fused_computation.5 | convolution fusion | flops 2127790080 | bytes 14607360 | tf_op jit(solution)/shard_map/sjcf,jfd->sjcd/dot_general | solution.py:48
  417.3 4.9 all-to-all-start.2
  422.2 0.3 all-reduce.8.cloned.1.call-start
  422.4 0.1 reduce_sum.42
  422.6 0.1 copy.52
  422.8 0.1 copy.54
  422.9 132.2 %all-to-all-done.2 = bf16[32,32,2880]{2,1,0:T(8,128)(2,1)} async-done(((bf16[32,32,2880]{2,1,0:T(8,128)(2,1)}), bf16[32,32,2880]{2,1,0:T(8,128)(2,1)}, u32[]{:S(2)}, u32[]{:S(2)}) %all-to-all-start.2) | async-done | bytes 5898272 | tf_op jit(solution)/shard_map/all_to_all | solution.py:102
  555.1 10.2 %gather_fusion.1 = bf16[512,2880]{1,0:T(8,128)(2,1)} fusion(bf16[1024,2880]{1,0:T(8,128)(2,1)} %bitcast.24, s32[1024]{0:T(1024)S(1)} %pad_clamp_fusion), kind=kCustom, calls=%fused_computation.1 | custom fusion | bytes 5900288 | tf_op jit(solution)/shard_map/jit(_take)/gather | solution.py:103
  565.3 5.8 gather.15
  571.1 9.3 %multiply_reduce_fusion = bf16[128,2880]{1,0:T(8,128)(2,1)} fusion(f32[128,4]{1,0:T(8,128)S(1)} %copy.54, bf16[128,4,2880]{2,1,0:T(4,128)(2,1)} %gather.15, pred[128,4]{1,0:T(8,128)(4,1)S(1)} %copy.52), kind=kLoop, calls=%fused_computation.3 | loop fusion | flops 5529600 | bytes 3688960 | tf_op jit(solution)/shard_map/reduce_sum | solution.py:104
  580.5 163.5 %all-reduce.8.cloned.1.call-done = bf16[128,2880]{1,0:T(8,128)(2,1)} async-done(((bf16[128,2880]{1,0:T(8,128)(2,1)}), bf16[128,2880]{1,0:T(8,128)(2,1)}) %all-reduce.8.cloned.1.call-update) | async-done | bytes 737296
  744.0 1.5 add_convert_fusion
  (40 shorter events, 0.4 us)
Async XLA Ops:
  6.5 398.4 %copy-start = (bf16[1,180,2880]{2,1,0:T(8,128)(2,1)S(1)}, bf16[1,180,2880]{2,1,0:T(8,128)(2,1)}, u32[]{:S(2)}) copy-start(bf16[1,180,2880]{2,1,0:T(8,128)(2,1)} %param.23) | copy-start | bytes 3110404
  8.5 3.4 copy-start.4
  8.5 3.5 copy-start.8
  12.8 16.0 %copy-start.5 = (s32[128,4]{0,1:T(4,128)S(1)}, s32[128,4]{0,1:T(4,128)}, u32[]{:S(2)}) copy-start(s32[128,4]{0,1:T(4,128)} %param.19) | copy-start | bytes 6148
  12.9 26.3 %copy-start.2 = (bf16[128,2880]{0,1:T(8,128)(2,1)S(1)}, bf16[128,2880]{0,1:T(8,128)(2,1)}, u32[]{:S(2)}) copy-start(bf16[128,2880]{0,1:T(8,128)(2,1)} %param.17) | copy-start | bytes 2211844
  14.7 184.9 %copy-start.3 = (bf16[8,2880]{1,0:T(8,128)(2,1)S(1)}, bf16[8,2880]{1,0:T(8,128)(2,1)}, u32[]{:S(2)}) copy-start(bf16[8,2880]{1,0:T(8,128)(2,1)} %param.12) | copy-start | bytes 138244
  14.8 185.9 %copy-start.6 = (f32[2880]{0:T(1024)S(1)}, f32[2880]{0:T(1024)}, u32[]{:S(2)}) copy-start(f32[2880]{0:T(1024)} %param.18) | copy-start | bytes 34564
  15.9 23.2 %all-to-all-start = ((bf16[8,16,128]{2,0,1:T(8,128)(2,1)}), bf16[8,16,128]{2,0,1:T(8,128)(2,1)S(1)}, u32[]{:S(2)}, u32[]{:S(2)}) async-start(bf16[8,16,128]{2,0,1:T(8,128)(2,1)} %copy.47), calls=%async_computation | async-start | bytes 65536 | tf_op jit(solution)/shard_map/all_to_all | solution.py:72
  28.8 170.8 %all-reduce.6.cloned.1.call-start = ((), (), s32[]{:S(2)}) async-start(), calls=%async_computation.3 | async-start | bytes 1507328
  256.0 146.1 %copy-start.9 = (bf16[1,2880,180]{1,2,0:T(8,128)(2,1)S(1)}, bf16[1,2880,180]{1,2,0:T(8,128)(2,1)}, u32[]{:S(2)}) copy-start(bf16[1,2880,180]{1,2,0:T(8,128)(2,1)} %param.21) | copy-start | bytes 3110404
  399.5 2.6 copy-start.1
  417.3 5.5 copy-start.7
  417.3 137.8 %all-to-all-start.2 = ((bf16[32,32,2880]{2,1,0:T(8,128)(2,1)}), bf16[32,32,2880]{2,1,0:T(8,128)(2,1)}, u32[]{:S(2)}, u32[]{:S(2)}) async-start(bf16[32,32,2880]{2,1,0:T(8,128)(2,1)} %convolution_convert_fusion), calls=%async_computation.2 | async-start | bytes 12058624 | tf_op jit(solution)/shard_map/all_to_all | solution.py:102
  422.2 321.8 %all-reduce.8.cloned.1.call-start = ((), (), s32[]{:S(2)}) async-start(), calls=%async_computation.4 | async-start | bytes 1507328
Sparse Core Ops, SparseCore 0:
  40.5 159.1 all-reduce.5
  580.6 163.3 all-reduce.7
where the time goes:
time: 753 us; the launch traced here: 752 us
  waiting for transfers between devices  459 us (61%)
  blocking collectives  188 us (25%)
  local copies, waits for them, and re-layouts  37.3 us (5%)
  matrix products  18.5 us (2%)
  starting transfers between devices  18.1 us (2%)
  other arithmetic  17.6 us (2%)
  between operations  14.3 us (2%)
    unnamed x4, waiting for transfers between devices  318 us
    all_to_all x1, blocking collectives, local(): lax.all_to_all(outgoing, 'exp', split_axis=0, concat_axis=0, tiled=True)  144 us
    all_to_all x1, waiting for transfers between devices, local(): lax.all_to_all(partial_value, 'exp', split_axis=0, concat_axis=0, tiled=T...  132 us
    all_gather x1, blocking collectives, local(): column = lax.all_gather(normed, 'attn', axis=0, tiled=True)  44.4 us
    gather x2, local copies, waits for them, and re-layouts, local(): jnp.take(returned.reshape(expert_total * capacity, returned.shape[2]), pl...  16 us
  transfers between devices with their start and end apart: 4, of which 4 were waited for; matrix products, arithmetic and copies ran while one was open for 1% of the time, Pallas kernels for 0%

commit v1 on v0

--- a/solution.py
+++ b/solution.py
@@ -88,7 +88,9 @@
     source_rows = (
         jnp.full((expert_total * capacity,), column_rows, jnp.int32).at[places].set(row_number)
     )
-    column = lax.all_gather(normed, "attn", axis=0, tiled=True)
+    column = jnp.concatenate(
+        lax.all_to_all(jnp.stack([normed] * lax.axis_size("attn")), "attn", 0, 0), axis=0
+    )
     padded = jnp.concatenate([column, jnp.zeros((1, column.shape[1]), jnp.bfloat16)], axis=0)
     outgoing = jnp.take(padded, source_rows, axis=0).reshape(
         expert_total, capacity, column.shape[1]

time: 753 us -> 730 us (0.969)
  blocking collectives: 188 us -> 166 us
    all_gather x1 -> x0, blocking collectives: 44.4 us -> none  [local(): column = lax.all_gather(normed, 'attn', axis=0, tiled=True)]
    all_to_all x0 -> x1, blocking collectives: none -> 23 us  [local(): lax.all_to_all(attention_output, 'attn', split_axis=1, concat_axis=0, til...]
where the time goes in v1:
time: 730 us; the launch traced here: 729 us
  waiting for transfers between devices  464 us (64%)
  blocking collectives  166 us (23%)
  local copies, waits for them, and re-layouts  37.6 us (5%)
  matrix products  18.2 us (2%)
  other arithmetic  17.6 us (2%)
  between operations  14.3 us (2%)
  starting transfers between devices  11.6 us (2%)
    unnamed x4, waiting for transfers between devices  319 us
    all_to_all x1, blocking collectives, local(): lax.all_to_all(outgoing, 'exp', split_axis=0, concat_axis=0, tiled=True)  143 us
    all_to_all x1, waiting for transfers between devices, local(): lax.all_to_all(partial_value, 'exp', split_axis=0, concat_axis=0, tiled=T...  132 us
    all_to_all x1, blocking collectives, local(): lax.all_to_all(attention_output, 'attn', split_axis=1, concat_axis=0, til...  23 us
    gather x2, local copies, waits for them, and re-layouts, local(): jnp.take(returned.reshape(expert_total * capacity, returned.shape[2]), pl...  16 us
  transfers between devices with their start and end apart: 4, of which 4 were waited for; matrix products, arithmetic and copies ran while one was open for 1% of the time, Pallas kernels for 0%

profile of v1, /device:TPU:8, one launch (start us, length us, event | category | flops | bytes accessed | tf_op | source)
XLA Modules:
  0.0 729.2 jit_solution(6351002878392564112)
XLA Ops:
  6.5 0.9 fusion.42
  7.4 1.1 copy.43
  8.5 2.2 fusion.41
  10.7 1.2 copy.55
  11.9 0.1 reshape.145
  12.0 0.1 max.18
  12.1 0.3 copy.46
  12.4 0.4 copy.57
  12.9 1.6 fusion.43
  14.5 0.2 fusion.24
  14.8 0.4 convolution_convert_fusion.2
  15.2 0.1 convert_element_type.51
  15.3 23.0 %all_to_all.31 = bf16[8,16,128]{2,0,1:T(8,128)(2,1)S(1)} all-to-all(bf16[8,16,128]{2,0,1:T(8,128)(2,1)S(1)} %copy.47), channel_id=1, replica_groups=mesh['attn'=16,'exp'=32] {'attn'}, dimensions={1} | all-to-all | bytes 65536 | tf_op jit(solution)/shard_map/all_to_all | solution.py:72
  38.3 1.2 convolution_convert_fusion.1
  39.6 0.1 copy.48
  39.7 0.1 eq.26
  39.8 0.1 reshape.146
  39.9 1.3 dynamic-slice
  41.8 156.9 %all-reduce.6.cloned.1.call-done = bf16[128,2880]{1,0:T(8,128)(2,1)} async-done(((bf16[128,2880]{1,0:T(8,128)(2,1)}), bf16[128,2880]{1,0:T(8,128)(2,1)}) %all-reduce.6.cloned.1.call-update) | async-done | bytes 737296
  198.7 0.9 multiply_reduce_fusion.1
  199.7 0.9 multiply_convert_fusion
  200.6 0.9 stack.2
  201.5 6.4 all-to-all-start.1
  208.0 1.2 reduce-window.6
  209.1 0.2 slice_reduce_fusion
  209.4 0.1 copy.53
  209.5 0.1 mul.76
  209.6 0.1 fusion.28
  209.7 2.4 scatter_custom_fusion
  212.2 0.1 broadcast_in_dim.45
  212.3 12.8 %all-to-all-done.1 = bf16[16,8,2880]{2,1,0:T(8,128)(2,1)S(1)} async-done(((bf16[16,8,2880]{2,1,0:T(8,128)(2,1)}), bf16[16,8,2880]{2,1,0:T(8,128)(2,1)S(1)}, u32[]{:S(2)}, u32[]{:S(2)}) %all-to-all-start.1) | async-done | bytes 737312 | tf_op jit(solution)/shard_map/all_to_all | solution.py:92
  225.2 6.5 gather_fusion
  231.7 3.4 broadcast_select_fusion
  235.1 143.1 %all_to_all.32 = bf16[32,32,2880]{2,1,0:T(8,128)(2,1)S(1)} all-to-all(bf16[32,32,2880]{2,1,0:T(8,128)(2,1)S(1)} %broadcast_select_fusion), channel_id=1, replica_groups=mesh['attn'=16,'exp'=32] {'exp'}, dimensions={0} | all-to-all | bytes 11796480 | tf_op jit(solution)/shard_map/all_to_all | solution.py:99
  378.2 2.6 copy-done.1
  380.8 2.8 convolution_bitcast_fusion
  383.6 12.1 %convolution_convert_fusion = bf16[32,32,2880]{2,1,0:T(8,128)(2,1)} fusion(bf16[32,32,2880]{2,1,0:T(8,128)(2,1)} %copy-done.1, bf16[1,180,2880]{2,1,0:T(8,128)(2,1)S(1)} %copy-done, bf16[1,2880,180]{1,2,0:T(8,128)(2,1)S(1)} %copy-done.10, f32[32,1,32,180]{3,2,0,1:T(8,128)} %convolution_bitcast_fusion), kind=kOutput, calls=%fused_computation.5 | convolution fusion | flops 2127790080 | bytes 14607360 | tf_op jit(solution)/shard_map/sjcf,jfd->sjcd/dot_general | solution.py:48
  395.7 4.9 all-to-all-start.3
  400.6 0.3 all-reduce.8.cloned.1.call-start
  400.9 0.1 reduce_sum.42
  401.1 0.1 copy.52
  401.2 0.1 copy.54
  401.4 132.2 %all-to-all-done.3 = bf16[32,32,2880]{2,1,0:T(8,128)(2,1)} async-done(((bf16[32,32,2880]{2,1,0:T(8,128)(2,1)}), bf16[32,32,2880]{2,1,0:T(8,128)(2,1)}, u32[]{:S(2)}, u32[]{:S(2)}) %all-to-all-start.3) | async-done | bytes 5898272 | tf_op jit(solution)/shard_map/all_to_all | solution.py:104
  533.5 10.2 %gather_fusion.1 = bf16[512,2880]{1,0:T(8,128)(2,1)} fusion(bf16[1024,2880]{1,0:T(8,128)(2,1)} %bitcast.25, s32[1024]{0:T(1024)S(1)} %pad_clamp_fusion), kind=kCustom, calls=%fused_computation.1 | custom fusion | bytes 5900288 | tf_op jit(solution)/shard_map/jit(_take)/gather | solution.py:105
  543.7 5.8 gather.15
  549.6 9.3 %multiply_reduce_fusion = bf16[128,2880]{1,0:T(8,128)(2,1)} fusion(f32[128,4]{1,0:T(8,128)S(1)} %copy.54, bf16[128,4,2880]{2,1,0:T(4,128)(2,1)} %gather.15, pred[128,4]{1,0:T(8,128)(4,1)S(1)} %copy.52), kind=kLoop, calls=%fused_computation.3 | loop fusion | flops 5529600 | bytes 3688960 | tf_op jit(solution)/shard_map/reduce_sum | solution.py:106
  558.9 162.0 %all-reduce.8.cloned.1.call-done = bf16[128,2880]{1,0:T(8,128)(2,1)} async-done(((bf16[128,2880]{1,0:T(8,128)(2,1)}), bf16[128,2880]{1,0:T(8,128)(2,1)}) %all-reduce.8.cloned.1.call-update) | async-done | bytes 737296
  720.9 1.5 add_convert_fusion
  (43 shorter events, 0.3 us)
Async XLA Ops:
  6.5 377.1 %copy-start = (bf16[1,180,2880]{2,1,0:T(8,128)(2,1)S(1)}, bf16[1,180,2880]{2,1,0:T(8,128)(2,1)}, u32[]{:S(2)}) copy-start(bf16[1,180,2880]{2,1,0:T(8,128)(2,1)} %param.23) | copy-start | bytes 3110404
  6.5 192.2 %all-reduce.6.cloned.1.call-start = ((), (), s32[]{:S(2)}) async-start(), calls=%async_computation.4 | async-start | bytes 1507328
  8.5 3.4 copy-start.4
  8.5 3.5 copy-start.8
  12.8 25.4 %copy-start.2 = (bf16[128,2880]{0,1:T(8,128)(2,1)S(1)}, bf16[128,2880]{0,1:T(8,128)(2,1)}, u32[]{:S(2)}) copy-start(bf16[128,2880]{0,1:T(8,128)(2,1)} %param.17) | copy-start | bytes 2211844
  14.5 25.1 %copy-start.5 = (s32[128,4]{0,1:T(4,128)S(1)}, s32[128,4]{0,1:T(4,128)}, u32[]{:S(2)}) copy-start(s32[128,4]{0,1:T(4,128)} %param.19) | copy-start | bytes 6148
  14.5 184.3 %copy-start.3 = (bf16[8,2880]{1,0:T(8,128)(2,1)S(1)}, bf16[8,2880]{1,0:T(8,128)(2,1)}, u32[]{:S(2)}) copy-start(bf16[8,2880]{1,0:T(8,128)(2,1)} %param.12) | copy-start | bytes 138244
  14.5 185.2 %copy-start.6 = (f32[2880]{0:T(1024)S(1)}, f32[2880]{0:T(1024)}, u32[]{:S(2)}) copy-start(f32[2880]{0:T(1024)} %param.18) | copy-start | bytes 34564
  201.5 23.6 %all-to-all-start.1 = ((bf16[16,8,2880]{2,1,0:T(8,128)(2,1)}), bf16[16,8,2880]{2,1,0:T(8,128)(2,1)S(1)}, u32[]{:S(2)}, u32[]{:S(2)}) async-start(bf16[16,8,2880]{2,1,0:T(8,128)(2,1)} %stack.2), calls=%async_computation.1 | async-start | bytes 1507328 | tf_op jit(solution)/shard_map/all_to_all | solution.py:92
  235.1 145.7 %copy-start.9 = (bf16[1,2880,180]{1,2,0:T(8,128)(2,1)S(1)}, bf16[1,2880,180]{1,2,0:T(8,128)(2,1)}, u32[]{:S(2)}) copy-start(bf16[1,2880,180]{1,2,0:T(8,128)(2,1)} %param.21) | copy-start | bytes 3110404
  378.2 2.6 copy-start.1
  380.8 2.8 copy-start.10
  395.7 5.5 copy-start.7
  395.7 137.8 %all-to-all-start.3 = ((bf16[32,32,2880]{2,1,0:T(8,128)(2,1)}), bf16[32,32,2880]{2,1,0:T(8,128)(2,1)}, u32[]{:S(2)}, u32[]{:S(2)}) async-start(bf16[32,32,2880]{2,1,0:T(8,128)(2,1)} %convolution_convert_fusion), calls=%async_computation.3 | async-start | bytes 12058624 | tf_op jit(solution)/shard_map/all_to_all | solution.py:104
  400.6 320.3 %all-reduce.8.cloned.1.call-start = ((), (), s32[]{:S(2)}) async-start(), calls=%async_computation.5 | async-start | bytes 1507328
Sparse Core Ops, SparseCore 0:
  39.7 159.0 all-reduce.5
  559.0 161.8 all-reduce.7
